TPU v7x, 512 devices: a whole 4x4x16 slice. The times are simulated.
512 devices in a mesh: vocab: 128 (over x, z, core), batch: 4 (over y).
Axes of the slice: x: 4, y: 4, z: 16, core: 2. Of those that a mesh axis runs over, the one named last changes fastest.
Arguments:
- hidden: bfloat16 [4096, 1024], P(('vocab', 'batch'))
- embedding: bfloat16 [131072, 1024], P('vocab')
- block_counts: int32 [1024], P('vocab'), may hold values from 1 to 4095
- lang_blocks: int32 [200, 64], replicated, may hold values from -1 to 1023, as said below
- sent_lang: int32 [64], replicated, may hold values from 0 to 199
- targets: int32 [4096], replicated, may hold values from 0 to 131071, as said below
Outputs:
- token_loss: float32 [4096], P(('vocab', 'batch'))
- grad_embed: bfloat16 [131072, 1024], P(('vocab', 'batch'))
Inputs may be any that keep to these rules, and one draw needn't show every extreme that they name: `lang_blocks`: each list holds distinct block numbers and then -1 padding; the first entry of every list is block 0; at least 16 entries are blocks, and some language fills all 64 entries. `targets`: the target of token t lies in a block listed for the language of sentence t // 64.
All inputs are finite; a program needn't handle non-finite values.
Results may differ from a plain program's by a relative error of at most 0.0075.
Values may be sent and summed in bfloat16 or wider, within the bound.
A program may use at most 64 MiB of HBM per device.

v0:
```python
import jax
import jax.numpy as jnp
from jax import lax
from jax.sharding import PartitionSpec as P

SEQ = 64
masked_fill = -1e30


def body(hidden, embedding, block_counts, lang_blocks, sent_lang, targets):
    tok_dev = hidden.shape[0]
    vocab_count = lax.axis_size("vocab")
    batch_count = lax.axis_size("batch")
    vocab_index = lax.axis_index("vocab")
    batch_index = lax.axis_index("batch")
    local_rows = embedding.shape[0]
    local_blocks = block_counts.shape[0]
    block_width = local_rows // local_blocks
    gathered = lax.all_gather(hidden, "vocab", axis=0, tiled=True)
    token_count = gathered.shape[0]
    token_ids = (
        (jnp.arange(vocab_count, dtype=jnp.int32)[:, None] * batch_count + batch_index) * tok_dev
        + jnp.arange(tok_dev, dtype=jnp.int32)[None, :]
    ).reshape(-1)
    target_ids = lax.dynamic_index_in_dim(
        targets.reshape(vocab_count, batch_count, tok_dev), batch_index, 1, keepdims=False
    ).reshape(-1)
    sentence = token_ids // SEQ
    sentence_hit = sentence[:, None] == jnp.arange(sent_lang.shape[0], dtype=jnp.int32)[None, :]
    token_language = jnp.sum(jnp.where(sentence_hit, sent_lang[None, :], 0), axis=1)
    block_ids = vocab_index * local_blocks + jnp.arange(local_blocks, dtype=jnp.int32)
    member = jnp.any(lang_blocks[:, :, None] == block_ids[None, None, :], axis=1).astype(
        jnp.float32
    )
    language_hit = (
        token_language[:, None] == jnp.arange(lang_blocks.shape[0], dtype=jnp.int32)[None, :]
    ).astype(jnp.float32)
    allowed = jnp.dot(language_hit, member, precision=lax.Precision.HIGHEST) > 0.5
    allowed_cells = allowed[:, :, None]
    raw_scores = lax.dot_general(
        gathered, embedding, (((1,), (1,)), ((), ())), preferred_element_type=jnp.float32
    )
    log_sampling = jnp.log(block_counts.astype(jnp.float32))
    logits = (
        raw_scores.reshape(token_count, local_blocks, block_width) - log_sampling[None, :, None]
    )
    masked = jnp.where(allowed_cells, logits, masked_fill)
    word_ids = (vocab_index * local_rows + jnp.arange(local_rows, dtype=jnp.int32)).reshape(
        local_blocks, block_width
    )
    is_target = word_ids[None, :, :] == target_ids[:, None, None]
    local_peak = jnp.max(masked, axis=(1, 2))
    local_target = jnp.sum(jnp.where(is_target, logits, 0.0), axis=(1, 2))
    peak_value = lax.pmax(local_peak, "vocab")
    local_total = jnp.sum(
        jnp.where(allowed_cells, jnp.exp(masked - peak_value[:, None, None]), 0.0), axis=(1, 2)
    )
    denominator, target_logit = lax.psum((local_total, local_target), "vocab")
    log_total = peak_value + jnp.log(denominator)
    every_loss = log_total - target_logit
    token_loss = lax.dynamic_slice_in_dim(every_loss, vocab_index * tok_dev, tok_dev, 0)
    softmax_weights = jnp.where(allowed_cells, jnp.exp(logits - log_total[:, None, None]), 0.0)
    grad_logits = (
        (softmax_weights - is_target.astype(jnp.float32))
        .astype(jnp.bfloat16)
        .reshape(token_count, local_rows)
    )
    partial_value = lax.dot_general(
        grad_logits, gathered, (((0,), (0,)), ((), ())), preferred_element_type=jnp.float32
    )
    rounded_terms = partial_value.astype(jnp.bfloat16)
    grad_embed = (
        lax.psum_scatter(rounded_terms, "batch", scatter_dimension=0, tiled=True)
        .astype(jnp.float32)
        .astype(jnp.bfloat16)
    )
    return (token_loss, grad_embed)


def solution(mesh):
    in_specs = (P(("vocab", "batch"), None), P("vocab", None), P("vocab"), P(), P(), P())
    out_specs = (P(("vocab", "batch")), P(("vocab", "batch"), None))
    return jax.shard_map(body, mesh=mesh, in_specs=in_specs, out_specs=out_specs, check_vma=False)
```

profile of v0, /device:TPU:1, one launch (start us, length us, event | category | flops | bytes accessed | tf_op | source)
XLA Modules:
  0.0 706.7 jit_solution(17756853080807426681)
XLA Ops:
  7.2 0.0 copy-start
  7.2 0.0 all-gather.2.cloned.1.call-start
  7.2 0.7 all-gather.2.cloned.1.call-update
  7.9 0.0 reduce-scatter.2.cloned.1.call-start
  8.0 0.1 iota_add_fusion
  8.1 0.1 add.86
  8.2 1.1 reshape.84
  9.2 0.2 dynamic-slice_reduce_fusion
  9.4 0.1 eq.66
  9.6 0.8 select_reduce_fusion
  10.3 1.0 compare_reduce_fusion
  11.3 0.7 convert_log_fusion
  12.0 0.1 broadcast_bitcast_fusion
  12.1 0.4 convolution_compare_fusion
  12.4 144.3 %all-gather.2.cloned.1.call-done = bf16[1024,1024]{1,0:T(8,128)(2,1)} async-done(((bf16[8,1024]{1,0:T(8,128)(2,1)}), bf16[1024,1024]{1,0:T(8,128)(2,1)}) %all-gather.2.cloned.1.call-update) | async-done | bytes 2097168 | tf_op jit(solution)/shard_map/all_gather | solution.py:19
  156.7 0.0 copy-done
  156.7 5.9 fusion.4
  162.6 246.4 %pmax.7 = f32[1024]{0:T(1024)S(1)} all-reduce(f32[1024]{0:T(1024)S(1)} %get-tuple-element.8), channel_id=1, replica_groups=mesh['vocab'=128,'batch'=4] {'vocab'}, use_global_device_ids=true, to_apply=%region_3.4 | all-reduce | flops 1024 | bytes 8192 | tf_op jit(solution)/shard_map/pmax | solution.py:54
  409.0 3.3 fusion
  412.3 254.4 %all-reduce = (f32[1024]{0:T(1024)S(1)}, f32[1024]{0:T(1024)S(1)}) all-reduce(f32[1024]{0:T(1024)S(1)} %get-tuple-element.3, f32[1024]{0:T(1024)S(1)} %get-tuple-element.2), channel_id=1, replica_groups=mesh['vocab'=128,'batch'=4] {'vocab'}, use_global_device_ids=true, to_apply=%region_5.6 | all-reduce | flops 2048 | bytes 16384 | tf_op jit(solution)/shard_map/psum | solution.py:58
  666.7 0.0 copy-start.1
  666.7 3.2 fusion.2
  669.9 0.0 copy-done.1
  669.9 3.7 convolution_convert_fusion
  673.6 0.0 reduce-scatter.2.cloned.1.call-update
  673.7 0.6 dynamic_slice.8
  674.3 25.6 %reduce-scatter.2.cloned.1.call-done = bf16[256,1024]{1,0:T(8,128)(2,1)} async-done(((bf16[1024,1024]{1,0:T(8,128)(2,1)}), bf16[256,1024]{1,0:T(8,128)(2,1)}) %reduce-scatter.2.cloned.1.call-update) | async-done | bytes 524304 | tf_op jit(solution)/shard_map/reduce_scatter | solution.py:73
  (5 shorter events, 0.0 us)
Async XLA Ops:
  7.2 149.5 %copy-start = (bf16[1024,1024]{1,0:T(8,128)(2,1)S(1)}, bf16[1024,1024]{1,0:T(8,128)(2,1)}, u32[]{:S(2)}) copy-start(bf16[1024,1024]{1,0:T(8,128)(2,1)} %param.7) | copy-start | bytes 6291460
  7.2 149.5 %all-gather.2.cloned.1.call-start = ((), (), s32[]{:S(2)}) async-start(), calls=%async_computation.1 | async-start | bytes 2113536 | tf_op jit(solution)/shard_map/all_gather | solution.py:19
  7.9 691.9 %reduce-scatter.2.cloned.1.call-start = ((), (), s32[]{:S(2)}) async-start(), calls=%async_computation.2 | async-start | bytes 2621440 | tf_op jit(solution)/shard_map/reduce_scatter | solution.py:73
  666.7 3.2 copy-start.1
Sparse Core Ops, SparseCore 0:
  11.1 145.4 all-gather.1
  673.8 26.0 reduce-scatter.1
where the time goes:
time: 707 us
  blocking collectives  501 us (71%)
  waiting for transfers between devices  171 us (24%)
  between operations  14.2 us (2%)
  matrix products  9.95 us (1%)
  other arithmetic  9.04 us (1%)
    psum x1, blocking collectives, body(): denominator, target_logit = lax.psum((local_total, local_target), 'vocab')  254 us
    pmax x1, blocking collectives, body(): peak_value = lax.pmax(local_peak, 'vocab')  246 us
    all_gather x1, waiting for transfers between devices, body(): gathered = lax.all_gather(hidden, 'vocab', axis=0, tiled=True)  144 us
    reduce_scatter x1, waiting for transfers between devices, body(): lax.psum_scatter(rounded_terms, 'batch', scatter_dimension=0, tiled=True)  25.6 us
  transfers between devices with their start and end apart: 2, of which 2 were waited for; matrix products, arithmetic and copies ran while one was open for 1% of the time, Pallas kernels for 0%

commit v1 on v0

--- a/solution.py
+++ b/solution.py
@@ -16,7 +16,10 @@
     local_rows = embedding.shape[0]
     local_blocks = block_counts.shape[0]
     block_width = local_rows // local_blocks
-    gathered = lax.all_gather(hidden, "vocab", axis=0, tiled=True)
+    count = lax.axis_size("vocab")
+    blocks = jnp.stack([hidden for _ in range(count)])
+    blocks = lax.all_to_all(blocks, "vocab", split_axis=0, concat_axis=0)
+    gathered = jnp.concatenate(blocks, axis=0)
     token_count = gathered.shape[0]
     token_ids = (
         (jnp.arange(vocab_count, dtype=jnp.int32)[:, None] * batch_count + batch_index) * tok_dev

time: 707 us -> 678 us (0.959)
  waiting for transfers between devices: 171 us -> 123 us
  starting transfers between devices: 0.08 us -> 20.9 us
    all_gather x1 -> x0, waiting for transfers between devices: 144 us -> none  [body(): gathered = lax.all_gather(hidden, 'vocab', axis=0, tiled=True)]
    all_to_all x0 -> x1, waiting for transfers between devices: none -> 97.2 us  [body(): blocks = lax.all_to_all(blocks, 'vocab', split_axis=0, concat_axis=0)]
    all_to_all x0 -> x1, starting transfers between devices: none -> 20.9 us  [body(): blocks = lax.all_to_all(blocks, 'vocab', split_axis=0, concat_axis=0)]
  transfers between devices with their start and end apart: 2 -> 2, of which waited for: 2 -> 2; matrix products, arithmetic and copies ran while one was open for 1% -> 0% of each run, Pallas kernels for 0% -> 0%
where the time goes in v1:
time: 678 us
  blocking collectives  498 us (73%)
  waiting for transfers between devices  123 us (18%)
  starting transfers between devices  20.9 us (3%)
  between operations  14.2 us (2%)
  matrix products  11.5 us (2%)
    psum x1, blocking collectives, body(): denominator, target_logit = lax.psum((local_total, local_target), 'vocab')  251 us
    pmax x1, blocking collectives, body(): peak_value = lax.pmax(local_peak, 'vocab')  247 us
    all_to_all x1, waiting for transfers between devices, body(): blocks = lax.all_to_all(blocks, 'vocab', split_axis=0, concat_axis=0)  97.2 us
    reduce_scatter x1, waiting for transfers between devices, body(): lax.psum_scatter(rounded_terms, 'batch', scatter_dimension=0, tiled=True)  25.8 us
    all_to_all x1, starting transfers between devices, body(): blocks = lax.all_to_all(blocks, 'vocab', split_axis=0, concat_axis=0)  20.9 us
  transfers between devices with their start and end apart: 2, of which 2 were waited for; matrix products, arithmetic and copies ran while one was open for 0% of the time, Pallas kernels for 0%

profile of v1, /device:TPU:1, one launch (start us, length us, event | category | flops | bytes accessed | tf_op | source)
XLA Modules:
  0.0 677.7 jit_solution(14025851545865825938)
XLA Ops:
  7.2 0.0 copy-start
  7.2 0.0 copy-start.2
  7.2 0.0 copy-start.3
  7.2 0.0 copy-start.1
  7.2 0.0 copy-start.4
  7.2 2.5 stack.2
  9.7 20.9 %all-to-all-start = ((bf16[128,8,1024]{2,1,0:T(8,128)(2,1)}), bf16[128,8,1024]{2,1,0:T(8,128)(2,1)}, u32[]{:S(2)}, u32[]{:S(2)}) async-start(bf16[128,8,1024]{2,1,0:T(8,128)(2,1)} %stack.2), calls=%async_computation | async-start | bytes 4194304 | tf_op jit(solution)/shard_map/all_to_all | solution.py:21
  30.6 0.0 reduce-scatter.2.cloned.1.call-start
  30.6 0.1 iota_add_fusion
  30.7 0.1 add.82
  30.8 0.0 copy-done.2
  30.8 0.3 reshape.76
  31.2 0.2 dynamic-slice_reduce_fusion
  31.4 0.1 eq.64
  31.5 0.0 copy-done.3
  31.5 0.1 select_reduce_fusion.2
  31.6 0.0 copy-done.1
  31.6 0.2 compare_reduce_fusion
  31.8 0.0 copy-done.4
  31.8 0.4 convolution_compare_fusion
  32.2 97.2 %all-to-all-done = bf16[128,8,1024]{2,1,0:T(8,128)(2,1)} async-done(((bf16[128,8,1024]{2,1,0:T(8,128)(2,1)}), bf16[128,8,1024]{2,1,0:T(8,128)(2,1)}, u32[]{:S(2)}, u32[]{:S(2)}) %all-to-all-start) | async-done | bytes 2097184 | tf_op jit(solution)/shard_map/all_to_all | solution.py:21
  129.3 0.0 copy-done
  129.3 5.9 select_reduce_fusion.1
  135.2 246.7 %pmax.7 = f32[1024]{0:T(1024)S(1)} all-reduce(f32[1024]{0:T(1024)S(1)} %get-tuple-element.8), channel_id=1, replica_groups=mesh['vocab'=128,'batch'=4] {'vocab'}, use_global_device_ids=true, to_apply=%region_3.4 | all-reduce | flops 1024 | bytes 8192 | tf_op jit(solution)/shard_map/pmax | solution.py:57
  382.0 3.3 fusion
  385.3 250.9 %all-reduce = (f32[1024]{0:T(1024)S(1)}, f32[1024]{0:T(1024)S(1)}) all-reduce(f32[1024]{0:T(1024)S(1)} %get-tuple-element.3, f32[1024]{0:T(1024)S(1)} %get-tuple-element.2), channel_id=1, replica_groups=mesh['vocab'=128,'batch'=4] {'vocab'}, use_global_device_ids=true, to_apply=%region_5.6 | all-reduce | flops 2048 | bytes 16384 | tf_op jit(solution)/shard_map/psum | solution.py:61
  636.2 3.0 fusion.2
  639.2 5.3 fusion.7
  644.5 0.0 reduce-scatter.2.cloned.1.call-update
  644.5 0.6 dynamic_slice.8
  645.1 25.8 %reduce-scatter.2.cloned.1.call-done = bf16[256,1024]{1,0:T(8,128)(2,1)} async-done(((bf16[1024,1024]{1,0:T(8,128)(2,1)}), bf16[256,1024]{1,0:T(8,128)(2,1)}) %reduce-scatter.2.cloned.1.call-update) | async-done | bytes 524304 | tf_op jit(solution)/shard_map/reduce_scatter | solution.py:76
  (6 shorter events, 0.0 us)
Async XLA Ops:
  7.2 122.2 %copy-start = (bf16[1024,1024]{1,0:T(8,128)(2,1)S(1)}, bf16[1024,1024]{1,0:T(8,128)(2,1)}, u32[]{:S(2)}) copy-start(bf16[1024,1024]{1,0:T(8,128)(2,1)} %param.7) | copy-start | bytes 6291460
  7.2 23.6 %copy-start.2 = (s32[4096]{0:T(1024)S(1)}, s32[4096]{0:T(1024)}, u32[]{:S(2)}) copy-start(s32[4096]{0:T(1024)} %param.11) | copy-start | bytes 49156
  7.2 24.3 %copy-start.3 = (s32[64]{0:T(128)S(1)}, s32[64]{0:T(128)}, u32[]{:S(2)}) copy-start(s32[64]{0:T(128)} %param.10) | copy-start | bytes 772
  7.2 24.4 %copy-start.1 = (s32[200,64]{0,1:T(8,128)S(1)}, s32[200,64]{0,1:T(8,128)}, u32[]{:S(2)}) copy-start(s32[200,64]{0,1:T(8,128)} %param.9) | copy-start | bytes 153604
  7.2 24.6 %copy-start.4 = (s32[8]{0:T(128)S(1)}, s32[8]{0:T(128)}, u32[]{:S(2)}) copy-start(s32[8]{0:T(128)} %param.8) | copy-start | bytes 100
  9.7 119.6 %all-to-all-start = ((bf16[128,8,1024]{2,1,0:T(8,128)(2,1)}), bf16[128,8,1024]{2,1,0:T(8,128)(2,1)}, u32[]{:S(2)}, u32[]{:S(2)}) async-start(bf16[128,8,1024]{2,1,0:T(8,128)(2,1)} %stack.2), calls=%async_computation | async-start | bytes 4194304 | tf_op jit(solution)/shard_map/all_to_all | solution.py:21
  30.6 640.3 %reduce-scatter.2.cloned.1.call-start = ((), (), s32[]{:S(2)}) async-start(), calls=%async_computation.2 | async-start | bytes 2621440 | tf_op jit(solution)/shard_map/reduce_scatter | solution.py:76
Sparse Core Ops, SparseCore 0:
  644.6 26.2 reduce-scatter.1
